TPU v7x, 32 devices: a whole 2x2x4 slice. The times are simulated.
32 devices in a mesh: wide: 8 (over y, x, core), narrow: 4 (over z).
Axes of the slice: x: 2, y: 2, z: 4, core: 2. Of those that a mesh axis runs over, the one named last changes fastest.
Arguments:
- amplitudes: bfloat16 [256, 4, 4096], P('wide', None, 'narrow'), may hold values from -6 to 6
- amp_tiles: int32 [8, 4], replicated, may hold values from 0 to 7, all different within a row
- integrals: bfloat16 [8, 2, 4096, 4096], P('wide', None, None, 'narrow'), may hold values from -0.09375 to 0.09375
- cd_tiles: int32 [8, 2], replicated, may hold values from 0 to 7, all different within a row
- q_owner: int32 [8], replicated, may hold values from 0 to 7, each once
Outputs:
- residual: bfloat16 [256, 8, 4096], P('wide', None, 'narrow')
Inputs may be any that keep to these rules, and one draw needn't show every extreme that they name: `amp_tiles`: within a row, the 4 tiles are different. `cd_tiles`: within a row, the 2 tiles are different; every tile is named by some row. `q_owner`: each owner index appears once.
All inputs are finite; a program needn't handle non-finite values.
Results may differ from a plain program's by a relative error of at most 0.017.
Values may be sent and summed in bfloat16 or wider, within the bound.
No kernel may reach another device: no remote copies, remote signals or barrier semaphores. Data moves between devices by JAX's collectives and lax.ppermute only.
A program may use at most 64 MiB of HBM per device.

v0:
```python
import jax
import jax.numpy as jnp
from jax import lax
from jax.sharding import PartitionSpec as P


def on_device(amplitudes, amp_tiles, integrals, cd_tiles, q_owner):
    my_index = lax.axis_index("wide")
    blocks = lax.axis_size("wide")
    rows_dev = amplitudes.shape[0]
    local_ints = integrals[0]
    tile_ids = jnp.arange(q_owner.shape[0], dtype=jnp.int32)
    holder = (q_owner[None, :] == jnp.arange(blocks, dtype=jnp.int32)[:, None]).astype(jnp.int32)
    owned_tile = jnp.sum(holder * tile_ids[None, :], axis=1)
    wanted = cd_tiles[owned_tile]
    my_wanted = wanted[my_index]
    segment = lax.all_gather(amplitudes, "wide", axis=0, tiled=True)
    length = segment.shape[0]
    source = jnp.arange(length, dtype=jnp.int32) // rows_dev
    tile_list = amp_tiles[source]
    picker = (tile_list[:, :, None] == my_wanted[None, None, :]).astype(jnp.bfloat16)
    chosen = jnp.einsum("rtk,rtc->rkc", picker, segment, preferred_element_type=jnp.float32).astype(
        jnp.bfloat16
    )
    partial_value = jnp.einsum(
        "rkc,kpc->rp", chosen, local_ints, preferred_element_type=jnp.float32
    )
    shares = lax.psum_scatter(
        partial_value.astype(jnp.bfloat16), "narrow", scatter_dimension=1, tiled=True
    )
    returned = lax.all_to_all(
        shares.reshape(blocks, rows_dev, shares.shape[1]),
        "wide",
        split_axis=0,
        concat_axis=0,
        tiled=True,
    )
    result = jnp.take(returned, q_owner, axis=0)
    return jnp.transpose(result, (1, 0, 2))


def solution(mesh):
    placed = (P("wide", None, "narrow"), P(), P("wide", None, None, "narrow"), P(), P())
    return jax.shard_map(
        on_device, mesh=mesh, in_specs=placed, out_specs=P("wide", None, "narrow"), check_vma=False
    )
```

profile of v0, /device:TPU:0, one launch (start us, length us, event | category | flops | bytes accessed | tf_op | source)
XLA Modules:
  0.0 127.0 jit_solution(11700073032151098230)
XLA Ops:
  6.5 0.0 all-gather.2.cloned.1.call-start
  6.5 0.7 all-gather.2.cloned.1.call-update
  7.3 0.0 reduce-scatter.2.cloned.1.call-start
  7.3 0.8 copy.16
  8.1 0.8 copy.15
  8.8 0.8 select_reduce_fusion
  9.6 0.6 gather_fusion.1
  10.2 0.7 gather_fusion
  10.9 28.9 %all-gather.2.cloned.1.call-done = bf16[256,4,1024]{2,1,0:T(4,128)(2,1)} async-done(((bf16[32,4,1024]{2,1,0:T(4,128)(2,1)}), bf16[256,4,1024]{2,1,0:T(4,128)(2,1)}) %all-gather.2.cloned.1.call-update) | async-done | bytes 2097168 | tf_op jit(solution)/shard_map/all_gather | solution.py:17
  39.9 2.9 %convolution_convert_fusion = bf16[256,2,1024]{2,1,0:T(2,128)(2,1)S(1)} fusion(bf16[256,4,1024]{2,1,0:T(4,128)(2,1)} %all-gather.2.cloned.1.call-done, s32[256,4]{1,0:T(8,128)S(1)} %gather_fusion, s32[2]{0:T(128)S(1)} %dynamic-slice_bitcast_fusion), kind=kOutput, calls=%fused_computation.7 | convolution fusion | flops 4720640 | bytes 3149832 | tf_op jit(solution)/shard_map/rtk,rtc->rkc/dot_general | solution.py:22
  42.8 18.1 %fusion.5 = bf16[256,4096]{1,0:T(8,128)(2,1)} fusion(bf16[1,2,4096,1024]{3,2,1,0:T(8,128)(2,1)} %param.7, bf16[256,2,1024]{2,1,0:T(2,128)(2,1)S(1)} %convolution_convert_fusion), kind=kOutput, calls=%fused_computation.6 | convolution fusion | flops 4296015872 | bytes 19922944 | tf_op jit(solution)/shard_map/rkc,kpc->rp/dot_general | solution.py:25
  60.9 0.0 copy-start
  60.9 0.0 reduce-scatter.2.cloned.1.call-update
  60.9 44.0 %reduce-scatter.2.cloned.1.call-done = bf16[256,1024]{1,0:T(8,128)(2,1)} async-done(((bf16[256,4096]{1,0:T(8,128)(2,1)}), bf16[256,1024]{1,0:T(8,128)(2,1)}) %reduce-scatter.2.cloned.1.call-update) | async-done | bytes 524304 | tf_op jit(solution)/shard_map/reduce_scatter | solution.py:28
  104.9 3.6 %all-to-all-start = ((bf16[8,32,1024]{2,1,0:T(8,128)(2,1)}), bf16[8,32,1024]{2,1,0:T(8,128)(2,1)S(1)}, u32[]{:S(2)}, u32[]{:S(2)}) async-start(bf16[8,32,1024]{2,1,0:T(8,128)(2,1)} %bitcast.22), calls=%async_computation.1 | async-start | bytes 1048576 | tf_op jit(solution)/shard_map/all_to_all | solution.py:31
  108.6 0.0 copy-done
  108.6 9.7 %all-to-all-done = bf16[8,32,1024]{2,1,0:T(8,128)(2,1)S(1)} async-done(((bf16[8,32,1024]{2,1,0:T(8,128)(2,1)}), bf16[8,32,1024]{2,1,0:T(8,128)(2,1)S(1)}, u32[]{:S(2)}, u32[]{:S(2)}) %all-to-all-start) | async-done | bytes 524320 | tf_op jit(solution)/shard_map/all_to_all | solution.py:31
  118.3 0.6 gather_fusion.2
  118.9 0.1 select_bitcast_fusion
  119.0 1.1 copy.18
  (8 shorter events, 0.1 us)
Async XLA Ops:
  6.5 33.3 %all-gather.2.cloned.1.call-start = ((), (), s32[]{:S(2)}) async-start(), calls=%async_computation.2 | async-start | bytes 2359296 | tf_op jit(solution)/shard_map/all_gather | solution.py:17
  7.3 97.7 %reduce-scatter.2.cloned.1.call-start = ((), (), s32[]{:S(2)}) async-start(), calls=%async_computation.3 | async-start | bytes 2621440 | tf_op jit(solution)/shard_map/reduce_scatter | solution.py:28
  60.9 47.7 %copy-start = (s32[8]{0:T(128)S(1)}, s32[8]{0:T(128)}, u32[]{:S(2)}) copy-start(s32[8]{0:T(128)} %param.9) | copy-start | bytes 100
  104.9 13.4 %all-to-all-start = ((bf16[8,32,1024]{2,1,0:T(8,128)(2,1)}), bf16[8,32,1024]{2,1,0:T(8,128)(2,1)S(1)}, u32[]{:S(2)}, u32[]{:S(2)}) async-start(bf16[8,32,1024]{2,1,0:T(8,128)(2,1)} %bitcast.22), calls=%async_computation.1 | async-start | bytes 1048576 | tf_op jit(solution)/shard_map/all_to_all | solution.py:31
Sparse Core Ops, SparseCore 0:
  9.2 30.5 all-gather.1
  61.0 43.8 reduce-scatter.1
where the time goes:
time: 127 us
  waiting for transfers between devices  83.4 us (66%)
  matrix products  21 us (17%)
  between operations  13.5 us (11%)
  local copies, waits for them, and re-layouts  4.47 us (4%)
  starting transfers between devices  3.67 us (3%)
    reduce_scatter x1, waiting for transfers between devices, on_device(): lax.psum_scatter(partial_value.astype(jnp.bfloat16), 'narrow', scatter_di...  44 us
    all_gather x1, waiting for transfers between devices, on_device(): segment = lax.all_gather(amplitudes, 'wide', axis=0, tiled=True)  28.9 us
    dot_general x1, matrix products, on_device(): jnp.einsum('rkc,kpc->rp', chosen, local_ints, preferred_element_type=jnp....  18.1 us
    all_to_all x1, waiting for transfers between devices, on_device(): lax.all_to_all(shares.reshape(blocks, rows_dev, shares.shape[1]), 'wide',...  9.7 us
    all_to_all x1, starting transfers between devices, on_device(): lax.all_to_all(shares.reshape(blocks, rows_dev, shares.shape[1]), 'wide',...  3.63 us
    dot_general x1, matrix products, on_device(): jnp.einsum('rtk,rtc->rkc', picker, segment, preferred_element_type=jnp.fl...  2.88 us
  transfers between devices with their start and end apart: 3, of which 3 were waited for; matrix products, arithmetic and copies ran while one was open for 3% of the time, Pallas kernels for 0%

commit v1 on v0

v1 whole, which is shorter than its diff:
```python
import functools

import jax
import jax.numpy as jnp
from jax import lax
from jax.experimental import pallas as pl
from jax.experimental.pallas import tpu as pltpu
from jax.sharding import PartitionSpec as P

PART = 512


def pick_kernel(peers, amp_tiles, cd_tiles, q_owner, amps, *rest):
    outs, held, slots = rest[:peers], rest[peers], rest[peers + 1]
    rows, width, _ = amps.shape
    wants = cd_tiles.shape[1]
    me = lax.axis_index("wide")

    def look(q, carry):
        peer = q_owner[q] ^ me
        for k in range(wants):
            slot = jnp.int32(width)
            for t in range(width):
                slot = jnp.where(amp_tiles[me, t] == cd_tiles[q, k], t, slot)
            slots[peer, k] = slot
        return carry

    lax.fori_loop(0, peers, look, 0)
    for t in range(width):
        held[t] = amps[:, t, :]
    held[width] = jnp.zeros_like(held[width])
    for j in range(peers):
        for k in range(wants):
            outs[j][k] = held[slots[j, k]]


def pick(amplitudes, amp_tiles, cd_tiles, q_owner):
    rows, width, depth = amplitudes.shape
    peers, wants = cd_tiles.shape
    smem = pl.BlockSpec(memory_space=pltpu.SMEM)
    vmem = pl.BlockSpec(memory_space=pltpu.VMEM)
    return pl.pallas_call(
        functools.partial(pick_kernel, peers),
        out_shape=[jax.ShapeDtypeStruct((wants, rows, depth), jnp.bfloat16)] * peers,
        in_specs=[smem, smem, smem, vmem],
        out_specs=[vmem] * peers,
        scratch_shapes=[
            pltpu.VMEM((width + 1, rows, depth), jnp.bfloat16),
            pltpu.SMEM((peers, wants), jnp.int32),
        ],
        compiler_params=pltpu.CompilerParams(vmem_limit_bytes=48 << 20),
        name="pick",
    )(amp_tiles, cd_tiles, q_owner, amplitudes)


def product_kernel(count, flip, *refs):
    picked, ints, out, left = refs[:count], refs[count], refs[count + 1], refs[count + 2]
    rows = picked[0].shape[1]

    @pl.when(pl.program_id(0) == 0)
    def _():
        for i, ref in enumerate(picked):
            for k in range(ref.shape[0]):
                left[k, i * rows : (i + 1) * rows, :] = ref[k]

    total = None
    for k in range(left.shape[0]):
        term = lax.dot_general(
            left[k], ints[0, k], (((1,), (1,)), ((), ())), preferred_element_type=jnp.float32
        )
        total = term if total is None else total + term
    out[...] = total.astype(jnp.bfloat16)


def product(flip, picked, ints, near, shards):
    wants, rows, depth = picked[0].shape
    pairs = ints.shape[2]
    share = pairs // shards
    part = min(PART, share)
    steps = share // part
    count = len(picked)

    def at(i, flip):
        shard = jnp.where(flip[0] == 0, near, shards - 1 - near)
        return (0, 0, shard * steps + i, 0)

    return pl.pallas_call(
        functools.partial(product_kernel, count),
        out_shape=jax.ShapeDtypeStruct((count * rows, share), jnp.bfloat16),
        grid_spec=pltpu.PrefetchScalarGridSpec(
            num_scalar_prefetch=1,
            grid=(steps,),
            in_specs=[pl.BlockSpec((wants, rows, depth), lambda i, flip: (0, 0, 0))] * count
            + [pl.BlockSpec((1, wants, part, depth), at)],
            out_specs=pl.BlockSpec((count * rows, part), lambda i, flip: (0, i)),
            scratch_shapes=[pltpu.VMEM((wants, count * rows, depth), jnp.bfloat16)],
        ),
        compiler_params=pltpu.CompilerParams(vmem_limit_bytes=48 << 20),
        cost_estimate=pl.CostEstimate(
            flops=2 * count * rows * wants * depth * share,
            bytes_accessed=2 * wants * depth * share + 2 * count * rows * (share + wants * depth),
            transcendentals=0,
        ),
        name="product",
    )(flip, *picked, ints)


def add(*terms):
    return sum(t.astype(jnp.float32) for t in terms).astype(jnp.bfloat16)


def line_sum(own, place, devices):
    last = []
    held = {}
    for d in range(devices - 1, 0, -1):
        for i in range(d):
            near = d if i < devices // 2 else devices - 1 - d
            value = own[near] if i == 0 else add(own[near], held[i - 1, d])
            held[i, d] = lax.ppermute(
                value, "narrow", [(i, i + 1), (devices - 1 - i, devices - 2 - i)]
            )
        last.append(held[d - 1, d])
    mine = own[0]
    for e in range(1, devices // 2):
        mine = jnp.where(place == e, own[e], mine)
    return add(mine, *last)


def order_kernel(peers, q_owner, *refs):
    shares, out, held = refs[:peers], refs[peers], refs[peers + 1]
    me = lax.axis_index("wide")

    def tile_of(j):
        def look(q, found):
            return jnp.where(q_owner[q] == me ^ j, q, found)

        return lax.fori_loop(0, peers, look, jnp.int32(0))

    for j in range(peers):
        held[tile_of(j)] = shares[j][...]
    for q in range(peers):
        out[:, q, :] = held[q]


def order(q_owner, shares):
    peers = len(shares)
    rows, share = shares[0].shape
    vmem = pl.BlockSpec(memory_space=pltpu.VMEM)
    return pl.pallas_call(
        functools.partial(order_kernel, peers),
        out_shape=jax.ShapeDtypeStruct((rows, peers, share), jnp.bfloat16),
        in_specs=[pl.BlockSpec(memory_space=pltpu.SMEM)] + [vmem] * peers,
        out_specs=vmem,
        scratch_shapes=[pltpu.VMEM((peers, rows, share), jnp.bfloat16)],
        compiler_params=pltpu.CompilerParams(vmem_limit_bytes=48 << 20),
        name="order",
    )(q_owner, *shares)


def on_device(amplitudes, amp_tiles, integrals, cd_tiles, q_owner):
    peers = lax.axis_size("wide")
    devices = lax.axis_size("narrow")
    rows = amplitudes.shape[0]
    at = lax.axis_index("narrow")
    place = jnp.minimum(at, devices - 1 - at)
    flip = jnp.where(at < devices // 2, 0, 1).astype(jnp.int32).reshape(1)

    def swap(value, j):
        return lax.ppermute(value, "wide", [(w, w ^ j) for w in range(peers)])

    picked = pick(amplitudes, amp_tiles, cd_tiles, q_owner)
    picked = [swap(p, j) if j else p for j, p in enumerate(picked)]
    shares = []
    for first, end in ((0, 2), (2, peers)):
        group = picked[first:end]
        own = [None] * devices
        for near in range(devices - 1, -1, -1):
            own[near] = product(flip, group, integrals, near, devices)
        total = line_sum(own, place, devices)
        for j in range(first, end):
            block = lax.slice_in_dim(total, (j - first) * rows, (j - first + 1) * rows)
            shares.append(swap(block, j) if j else block)
    return order(q_owner, shares)


def solution(mesh):
    placed = (P("wide", None, "narrow"), P(), P("wide", None, None, "narrow"), P(), P())
    return jax.shard_map(
        on_device, mesh=mesh, in_specs=placed, out_specs=P("wide", None, "narrow"), check_vma=False
    )
```

time: 127 us -> 98.4 us (0.77)
  waiting for transfers between devices: 83.4 us -> 33.7 us
  Pallas kernels: 0 us -> 30.4 us
  starting transfers between devices: 3.67 us -> 29.4 us
  matrix products: 21 us -> 0 us
  between operations: 13.5 us -> 0.37 us
  local copies, waits for them, and re-layouts: 4.47 us -> 3.16 us
    reduce_scatter x1 -> x0, waiting for transfers between devices: 44 us -> none  [on_device(): lax.psum_scatter(partial_value.astype(jnp.bfloat16), 'narrow', scatter_di...]
    ppermute x0 -> x26, waiting for transfers between devices: none -> 33.7 us  [the longest x12 29.1 us: line_sum(): lax.ppermute(value, 'narrow', [(i, i + 1), (devices - 1 - i, devices - 2...]
    pallas_call x0 -> x10, Pallas kernels: none -> 30.4 us  [the longest x8 26.5 us: product(): pl.pallas_call(functools.partial(product_kernel, count), out_shape=jax.Sh...]
    ppermute x0 -> x26, starting transfers between devices: none -> 29.4 us  [the longest x12 15.3 us: line_sum(): lax.ppermute(value, 'narrow', [(i, i + 1), (devices - 1 - i, devices - 2...]
    all_gather x1 -> x0, waiting for transfers between devices: 28.9 us -> none  [on_device(): segment = lax.all_gather(amplitudes, 'wide', axis=0, tiled=True)]
    dot_general x2 -> x0, matrix products: 21 us -> none  [the longest x1 18.1 us: on_device(): jnp.einsum('rkc,kpc->rp', chosen, local_ints, preferred_element_type=jnp....]
    all_to_all x1 -> x0, waiting for transfers between devices: 9.7 us -> none  [on_device(): lax.all_to_all(shares.reshape(blocks, rows_dev, shares.shape[1]), 'wide',...]
    all_to_all x1 -> x0, starting transfers between devices: 3.63 us -> none  [on_device(): lax.all_to_all(shares.reshape(blocks, rows_dev, shares.shape[1]), 'wide',...]
  transfers between devices with their start and end apart: 3 -> 26, of which waited for: 3 -> 9; matrix products, arithmetic and copies ran while one was open for 3% -> 1% of each run, Pallas kernels for 0% -> 27%
where the time goes in v1:
time: 98.4 us; the launch traced here: 98 us
  waiting for transfers between devices  33.7 us (34%)
  Pallas kernels  30.4 us (31%)
  starting transfers between devices  29.4 us (30%)
  local copies, waits for them, and re-layouts  3.16 us (3%)
    ppermute x12, waiting for transfers between devices, line_sum(): lax.ppermute(value, 'narrow', [(i, i + 1), (devices - 1 - i, devices - 2...  29.1 us
    pallas_call x8, Pallas kernels, product(): pl.pallas_call(functools.partial(product_kernel, count), out_shape=jax.Sh...  26.5 us
    ppermute x12, starting transfers between devices, line_sum(): lax.ppermute(value, 'narrow', [(i, i + 1), (devices - 1 - i, devices - 2...  15.3 us
    ppermute x14, starting transfers between devices, swap(): return lax.ppermute(value, 'wide', [(w, w ^ j) for w in range(peers)])  14.1 us
    ppermute x14, waiting for transfers between devices, swap(): return lax.ppermute(value, 'wide', [(w, w ^ j) for w in range(peers)])  4.63 us
    unnamed x8, local copies, waits for them, and re-layouts  3.12 us
    pallas_call x1, Pallas kernels, order(): pl.pallas_call(functools.partial(order_kernel, peers), out_shape=jax.Shap...  2.49 us
  transfers between devices with their start and end apart: 26, of which 9 were waited for; matrix products, arithmetic and copies ran while one was open for 1% of the time, Pallas kernels for 27%

profile of v1, /device:TPU:0, one launch (start us, length us, event | category | flops | bytes accessed | tf_op | source)
XLA Modules:
  0.0 98.0 jit_solution(4418039412391436286)
XLA Ops:
  0.0 0.8 copy.6.amp_tiles
  0.8 0.8 copy.7.cd_tiles
  1.5 0.9 copy-done
  2.5 0.7 copy-done.1
  3.1 1.4 %pick.1 = (bf16[2,32,1024]{2,1,0:T(8,128)(2,1)S(1)}, bf16[2,32,1024]{2,1,0:T(8,128)(2,1)S(1)}, bf16[2,32,1024]{2,1,0:T(8,128)(2,1)S(1)}, bf16[2,32,1024]{2,1,0:T...) custom-call(s32[8,4]{1,0:T(8,128)S(1)} %copy.6.amp_tiles, ...), custom_call_target="tpu_custom_call" | custom-call | tf_op jit(solution)/shard_map/pick/pallas_call | solution.py:42
  4.5 0.5 collective-permute-start
  5.1 2.6 %collective-permute-start.8 = (bf16[2,32,1024]{2,1,0:T(8,128)(2,1)S(1)}, bf16[2,32,1024]{2,1,0:T(8,128)(2,1)S(1)}, u32[]{:S(2)}, u32[]{:S(2)}) collective-permute-start(bf16[2,32,1024]{2,1,0:T(8,128)(2,1)S(1)} %get-tuple-element.15), channel_id=1, source_target_pairs={{0,8},{4,12},{8,0},{12,4},{16,24},{20,28},{24,16},{28,20},{1,9},{5... | collective-permute-start | bytes 393224 | tf_op jit(solution)/shard_map/ppermute | solution.py:169
  7.7 1.8 %collective-permute-start.10 = (bf16[2,32,1024]{2,1,0:T(8,128)(2,1)S(1)}, bf16[2,32,1024]{2,1,0:T(8,128)(2,1)S(1)}, u32[]{:S(2)}, u32[]{:S(2)}) collective-permute-start(bf16[2,32,1024]{2,1,0:T(8,128)(2,1)S(1)} %get-tuple-element.17), channel_id=1, source_target_pairs={{0,16},{4,20},{8,24},{12,28},{16,0},{20,4},{24,8},{28,12},{1,17},{... | collective-permute-start | bytes 393224 | tf_op jit(solution)/shard_map/ppermute | solution.py:169
  9.5 2.6 %collective-permute-start.12 = (bf16[2,32,1024]{2,1,0:T(8,128)(2,1)S(1)}, bf16[2,32,1024]{2,1,0:T(8,128)(2,1)S(1)}, u32[]{:S(2)}, u32[]{:S(2)}) collective-permute-start(bf16[2,32,1024]{2,1,0:T(8,128)(2,1)S(1)} %get-tuple-element.19), channel_id=1, source_target_pairs={{0,24},{4,28},{8,16},{12,20},{16,8},{20,12},{24,0},{28,4},{1,25},{... | collective-permute-start | bytes 393224 | tf_op jit(solution)/shard_map/ppermute | solution.py:169
  12.1 1.6 %collective-permute-start.13 = (bf16[2,32,1024]{2,1,0:T(8,128)(2,1)S(1)}, bf16[2,32,1024]{2,1,0:T(8,128)(2,1)S(1)}, u32[]{:S(2)}, u32[]{:S(2)}) collective-permute-start(bf16[2,32,1024]{2,1,0:T(8,128)(2,1)S(1)} %get-tuple-element.20), channel_id=1, source_target_pairs={{0,28},{4,24},{8,20},{12,16},{16,12},{20,8},{24,4},{28,0},{1,29},{... | collective-permute-start | bytes 393224 | tf_op jit(solution)/shard_map/ppermute | solution.py:169
  13.7 3.2 %product.11 = bf16[64,1024]{1,0:T(8,128)(2,1)S(1)} custom-call(s32[1]{0:T(128)} %bitcast.flip, bf16[2,32,1024]{2,1,0:T(8,128)(2,1)S(1)} %get-tuple-element.13.refs_0_, bf16[2,32,1024]{2,1,0:T(8,128)(2,1)S(1)} %collective-permute-done.refs_1_, bf16[1,2,4096,1024]{3,2,1,0:T(8,128)(2,1)} %refs_6_.7), custom_call_target="tpu_custom_call" | custom-call | flops 268435456 | bytes 4587520 | tf_op jit(solution)/shard_map/product/pallas_call | solution.py:87
  16.9 3.2 %product.10 = bf16[64,1024]{1,0:T(8,128)(2,1)S(1)} custom-call(s32[1]{0:T(128)} %bitcast.flip, bf16[2,32,1024]{2,1,0:T(8,128)(2,1)S(1)} %get-tuple-element.13.refs_0_, bf16[2,32,1024]{2,1,0:T(8,128)(2,1)S(1)} %collective-permute-done.refs_1_, bf16[1,2,4096,1024]{3,2,1,0:T(8,128)(2,1)} %refs_6_.7), custom_call_target="tpu_custom_call" | custom-call | flops 268435456 | bytes 4587520 | tf_op jit(solution)/shard_map/product/pallas_call | solution.py:87
  20.1 3.2 %product.8 = bf16[64,1024]{1,0:T(8,128)(2,1)S(1)} custom-call(s32[1]{0:T(128)} %bitcast.flip, bf16[2,32,1024]{2,1,0:T(8,128)(2,1)S(1)} %get-tuple-element.13.refs_0_, bf16[2,32,1024]{2,1,0:T(8,128)(2,1)S(1)} %collective-permute-done.refs_1_, bf16[1,2,4096,1024]{3,2,1,0:T(8,128)(2,1)} %refs_6_.7), custom_call_target="tpu_custom_call" | custom-call | flops 268435456 | bytes 4587520 | tf_op jit(solution)/shard_map/product/pallas_call | solution.py:87
  23.3 3.5 %collective-permute-start.6 = (bf16[64,1024]{1,0:T(8,128)(2,1)S(1)}, bf16[64,1024]{1,0:T(8,128)(2,1)S(1)}, u32[]{:S(2)}, u32[]{:S(2)}) collective-permute-start(bf16[64,1024]{1,0:T(8,128)(2,1)S(1)} %product.8), channel_id=1, source_target_pairs={{0,1},{3,2},{4,5},{7,6},{8,9},{11,10},{12,13},{15,14},{16,17},{19,... | collective-permute-start | bytes 393224 | tf_op jit(solution)/shard_map/ppermute | solution.py:119
  26.8 1.3 %collective-permute-start.1 = (bf16[64,1024]{1,0:T(8,128)(2,1)S(1)}, bf16[64,1024]{1,0:T(8,128)(2,1)S(1)}, u32[]{:S(2)}, u32[]{:S(2)}) collective-permute-start(bf16[64,1024]{1,0:T(8,128)(2,1)S(1)} %product.10), channel_id=1, source_target_pairs={{0,1},{3,2},{4,5},{7,6},{8,9},{11,10},{12,13},{15,14},{16,17},{19,... | collective-permute-start | bytes 393224 | tf_op jit(solution)/shard_map/ppermute | solution.py:119
  28.1 1.3 %collective-permute-start.4 = (bf16[64,1024]{1,0:T(8,128)(2,1)S(1)}, bf16[64,1024]{1,0:T(8,128)(2,1)S(1)}, u32[]{:S(2)}, u32[]{:S(2)}) collective-permute-start(bf16[64,1024]{1,0:T(8,128)(2,1)S(1)} %product.11), channel_id=1, source_target_pairs={{0,1},{3,2},{4,5},{7,6},{8,9},{11,10},{12,13},{15,14},{16,17},{19,... | collective-permute-start | bytes 393224 | tf_op jit(solution)/shard_map/ppermute | solution.py:119
  29.4 3.4 %product.12 = bf16[192,1024]{1,0:T(8,128)(2,1)S(1)} custom-call(s32[1]{0:T(128)} %bitcast.flip, bf16[2,32,1024]{2,1,0:T(8,128)(2,1)S(1)} %collective-permute-done.8.refs_0_, bf16[2,32,1024]{2,1,0:T(8,128)(2,1)S(1)} %collective-permute-done.9.refs_1_, bf16[2,32,1024]{2,1,0:T(8,128)(2,1)S(1)} %collective-permute-done.10.refs_2_, ...), custom_call_target="tpu_custom_call" | custom-call | flops 805306368 | bytes 5373952 | tf_op jit(solution)/shard_map/product/pallas_call | solution.py:87
  32.9 1.3 %collective-permute-start.19 = (bf16[192,1024]{1,0:T(8,128)(2,1)S(1)}, bf16[192,1024]{1,0:T(8,128)(2,1)S(1)}, u32[]{:S(2)}, u32[]{:S(2)}) collective-permute-start(bf16[192,1024]{1,0:T(8,128)(2,1)S(1)} %product.12), channel_id=1, source_target_pairs={{0,1},{3,2},{4,5},{7,6},{8,9},{11,10},{12,13},{15,14},{16,17},{19,... | collective-permute-start | bytes 1179656 | tf_op jit(solution)/shard_map/ppermute | solution.py:119
  34.2 3.4 %product.14 = bf16[192,1024]{1,0:T(8,128)(2,1)S(1)} custom-call(s32[1]{0:T(128)} %bitcast.flip, bf16[2,32,1024]{2,1,0:T(8,128)(2,1)S(1)} %collective-permute-done.8.refs_0_, bf16[2,32,1024]{2,1,0:T(8,128)(2,1)S(1)} %collective-permute-done.9.refs_1_, bf16[2,32,1024]{2,1,0:T(8,128)(2,1)S(1)} %collective-permute-done.10.refs_2_, ...), custom_call_target="tpu_custom_call" | custom-call | flops 805306368 | bytes 5373952 | tf_op jit(solution)/shard_map/product/pallas_call | solution.py:87
  37.6 1.3 %collective-permute-start.14 = (bf16[192,1024]{1,0:T(8,128)(2,1)S(1)}, bf16[192,1024]{1,0:T(8,128)(2,1)S(1)}, u32[]{:S(2)}, u32[]{:S(2)}) collective-permute-start(bf16[192,1024]{1,0:T(8,128)(2,1)S(1)} %product.14), channel_id=1, source_target_pairs={{0,1},{3,2},{4,5},{7,6},{8,9},{11,10},{12,13},{15,14},{16,17},{19,... | collective-permute-start | bytes 1179656 | tf_op jit(solution)/shard_map/ppermute | solution.py:119
  38.9 3.2 %product.9 = bf16[64,1024]{1,0:T(8,128)(2,1)S(1)} custom-call(s32[1]{0:T(128)} %bitcast.flip, bf16[2,32,1024]{2,1,0:T(8,128)(2,1)S(1)} %get-tuple-element.13.refs_0_, bf16[2,32,1024]{2,1,0:T(8,128)(2,1)S(1)} %collective-permute-done.refs_1_, bf16[1,2,4096,1024]{3,2,1,0:T(8,128)(2,1)} %refs_6_.7), custom_call_target="tpu_custom_call" | custom-call | flops 268435456 | bytes 4587520 | tf_op jit(solution)/shard_map/product/pallas_call | solution.py:87
  42.1 3.4 %product.15 = bf16[192,1024]{1,0:T(8,128)(2,1)S(1)} custom-call(s32[1]{0:T(128)} %bitcast.flip, bf16[2,32,1024]{2,1,0:T(8,128)(2,1)S(1)} %collective-permute-done.8.refs_0_, bf16[2,32,1024]{2,1,0:T(8,128)(2,1)S(1)} %collective-permute-done.9.refs_1_, bf16[2,32,1024]{2,1,0:T(8,128)(2,1)S(1)} %collective-permute-done.10.refs_2_, ...), custom_call_target="tpu_custom_call" | custom-call | flops 805306368 | bytes 5373952 | tf_op jit(solution)/shard_map/product/pallas_call | solution.py:87
  45.6 3.4 %product.13 = bf16[192,1024]{1,0:T(8,128)(2,1)S(1)} custom-call(s32[1]{0:T(128)} %bitcast.flip, bf16[2,32,1024]{2,1,0:T(8,128)(2,1)S(1)} %collective-permute-done.8.refs_0_, bf16[2,32,1024]{2,1,0:T(8,128)(2,1)S(1)} %collective-permute-done.9.refs_1_, bf16[2,32,1024]{2,1,0:T(8,128)(2,1)S(1)} %collective-permute-done.10.refs_2_, ...), custom_call_target="tpu_custom_call" | custom-call | flops 805306368 | bytes 5373952 | tf_op jit(solution)/shard_map/product/pallas_call | solution.py:87
  49.0 1.3 %collective-permute-start.17 = (bf16[192,1024]{1,0:T(8,128)(2,1)S(1)}, bf16[192,1024]{1,0:T(8,128)(2,1)S(1)}, u32[]{:S(2)}, u32[]{:S(2)}) collective-permute-start(bf16[192,1024]{1,0:T(8,128)(2,1)S(1)} %product.15), channel_id=1, source_target_pairs={{0,1},{3,2},{4,5},{7,6},{8,9},{11,10},{12,13},{15,14},{16,17},{19,... | collective-permute-start | bytes 1179656 | tf_op jit(solution)/shard_map/ppermute | solution.py:119
  50.4 0.7 collective-permute-start.2
  51.1 1.6 %collective-permute-done.14 = bf16[192,1024]{1,0:T(8,128)(2,1)S(1)} collective-permute-done((bf16[192,1024]{1,0:T(8,128)(2,1)S(1)}, bf16[192,1024]{1,0:T(8,128)(2,1)S(1)}, u32[]{:S(2)}, u32[]{:S(2)}) %collective-permute-start.14) | collective-permute-done | bytes 393248 | tf_op jit(solution)/shard_map/ppermute | solution.py:119
  52.8 0.7 collective-permute-start.5
  53.4 0.1 add_convert_fusion.3
  53.6 0.7 collective-permute-start.15
  54.3 6.9 %collective-permute-done.17 = bf16[192,1024]{1,0:T(8,128)(2,1)S(1)} collective-permute-done((bf16[192,1024]{1,0:T(8,128)(2,1)S(1)}, bf16[192,1024]{1,0:T(8,128)(2,1)S(1)}, u32[]{:S(2)}, u32[]{:S(2)}) %collective-permute-start.17) | collective-permute-done | bytes 393248 | tf_op jit(solution)/shard_map/ppermute | solution.py:119
  61.2 1.3 %collective-permute-start.3 = (bf16[64,1024]{1,0:T(8,128)(2,1)S(1)}, bf16[64,1024]{1,0:T(8,128)(2,1)S(1)}, u32[]{:S(2)}, u32[]{:S(2)}) collective-permute-start(bf16[64,1024]{1,0:T(8,128)(2,1)S(1)} %add_convert_fusion.6), channel_id=1, source_target_pairs={{2,3},{1,0},{6,7},{5,4},{10,11},{9,8},{14,15},{13,12},{18,19},{17,... | collective-permute-start | bytes 393224 | tf_op jit(solution)/shard_map/ppermute | solution.py:119
  62.5 0.1 add_convert_fusion.1
  62.6 0.7 collective-permute-start.18
  63.3 0.1 add_convert_fusion.2
  63.5 1.3 %collective-permute-start.16 = (bf16[192,1024]{1,0:T(8,128)(2,1)S(1)}, bf16[192,1024]{1,0:T(8,128)(2,1)S(1)}, u32[]{:S(2)}, u32[]{:S(2)}) collective-permute-start(bf16[192,1024]{1,0:T(8,128)(2,1)S(1)} %add_convert_fusion.2), channel_id=1, source_target_pairs={{2,3},{1,0},{6,7},{5,4},{10,11},{9,8},{14,15},{13,12},{18,19},{17,... | collective-permute-start | bytes 1179656 | tf_op jit(solution)/shard_map/ppermute | solution.py:119
  64.8 4.1 %collective-permute-done.3 = bf16[64,1024]{1,0:T(8,128)(2,1)S(1)} collective-permute-done((bf16[64,1024]{1,0:T(8,128)(2,1)S(1)}, bf16[64,1024]{1,0:T(8,128)(2,1)S(1)}, u32[]{:S(2)}, u32[]{:S(2)}) %collective-permute-start.3) | collective-permute-done | bytes 131104 | tf_op jit(solution)/shard_map/ppermute | solution.py:119
  69.2 16.4 %collective-permute-done.16 = bf16[192,1024]{1,0:T(8,128)(2,1)S(1)} collective-permute-done((bf16[192,1024]{1,0:T(8,128)(2,1)S(1)}, bf16[192,1024]{1,0:T(8,128)(2,1)S(1)}, u32[]{:S(2)}, u32[]{:S(2)}) %collective-permute-start.16) | collective-permute-done | bytes 393248 | tf_op jit(solution)/shard_map/ppermute | solution.py:119
  85.6 0.3 add_convert_fusion
  86.0 1.6 %collective-permute-start.24 = (bf16[32,1024]{1,0:T(8,128)(2,1)S(1)}, bf16[32,1024]{1,0:T(8,128)(2,1)S(1)}, u32[]{:S(2)}, u32[]{:S(2)}) collective-permute-start(bf16[32,1024]{1,0:T(8,128)(2,1)S(1)} %get-tuple-element.22), channel_id=1, source_target_pairs={{0,24},{4,28},{8,16},{12,20},{16,8},{20,12},{24,0},{28,4},{1,25},{... | collective-permute-start | bytes 196616 | tf_op jit(solution)/shard_map/ppermute | solution.py:169
  87.6 1.3 %collective-permute-start.23 = (bf16[32,1024]{1,0:T(8,128)(2,1)S(1)}, bf16[32,1024]{1,0:T(8,128)(2,1)S(1)}, u32[]{:S(2)}, u32[]{:S(2)}) collective-permute-start(bf16[32,1024]{1,0:T(8,128)(2,1)S(1)} %get-tuple-element.23), channel_id=1, source_target_pairs={{0,20},{4,16},{8,28},{12,24},{16,4},{20,0},{24,12},{28,8},{1,21},{... | collective-permute-start | bytes 196616 | tf_op jit(solution)/shard_map/ppermute | solution.py:169
  88.9 1.5 %collective-permute-start.22 = (bf16[32,1024]{1,0:T(8,128)(2,1)S(1)}, bf16[32,1024]{1,0:T(8,128)(2,1)S(1)}, u32[]{:S(2)}, u32[]{:S(2)}) collective-permute-start(bf16[32,1024]{1,0:T(8,128)(2,1)S(1)} %get-tuple-element.24), channel_id=1, source_target_pairs={{0,16},{4,20},{8,24},{12,28},{16,0},{20,4},{24,8},{28,12},{1,17},{... | collective-permute-start | bytes 196616 | tf_op jit(solution)/shard_map/ppermute | solution.py:169
  90.4 0.3 collective-permute-done.25.refs_7_
  90.7 0.5 collective-permute-start.20
  91.2 0.8 collective-permute-done.24.refs_6_
  92.0 1.3 %collective-permute-done.23.refs_5_ = bf16[32,1024]{1,0:T(8,128)(2,1)S(1)} collective-permute-done((bf16[32,1024]{1,0:T(8,128)(2,1)S(1)}, bf16[32,1024]{1,0:T(8,128)(2,1)S(1)}, u32[]{:S(2)}, u32[]{:S(2)}) %collective-permute-start.23) | collective-permute-done | bytes 65568 | tf_op jit(solution)/shard_map/ppermute | solution.py:169
  93.3 1.5 %collective-permute-done.22.refs_4_ = bf16[32,1024]{1,0:T(8,128)(2,1)S(1)} collective-permute-done((bf16[32,1024]{1,0:T(8,128)(2,1)S(1)}, bf16[32,1024]{1,0:T(8,128)(2,1)S(1)}, u32[]{:S(2)}, u32[]{:S(2)}) %collective-permute-start.22) | collective-permute-done | bytes 65568 | tf_op jit(solution)/shard_map/ppermute | solution.py:169
  94.8 0.7 collective-permute-done.20.refs_2_
  95.5 2.5 %order.1 = bf16[32,8,1024]{2,1,0:T(8,128)(2,1)} custom-call(s32[8]{0:T(128)S(1)} %copy-done.2, bf16[32,1024]{1,0:T(8,128)(2,1)S(1)} %get-tuple-element.28.refs_0_, bf16[32,1024]{1,0:T(8,128)(2,1)S(1)} %collective-permute-done.7.refs_1_, bf16[32,1024]{1,0:T(8,128)(2,1)S(1)} %collective-permute-done.20.refs_2_, ...), custom_call_target="tpu_custom_call" | custom-call | tf_op jit(solution)/shard_map/order/pallas_call | solution.py:149
  (32 shorter events, 0.5 us)
Async XLA Ops:
  1.5 0.9 copy-start
  2.5 0.7 copy-start.1
  4.5 4.9 %collective-permute-start = (bf16[2,32,1024]{2,1,0:T(8,128)(2,1)S(1)}, bf16[2,32,1024]{2,1,0:T(8,128)(2,1)S(1)}, u32[]{:S(2)}, u32[]{:S(2)}) collective-permute-start(bf16[2,32,1024]{2,1,0:T(8,128)(2,1)S(1)} %get-tuple-element.14), channel_id=1, source_target_pairs={{0,4},{4,0},{8,12},{12,8},{16,20},{20,16},{24,28},{28,24},{1,5},{5... | collective-permute-start | bytes 393224 | tf_op jit(solution)/shard_map/ppermute | solution.py:169
  5.1 7.0 %collective-permute-start.8 = (bf16[2,32,1024]{2,1,0:T(8,128)(2,1)S(1)}, bf16[2,32,1024]{2,1,0:T(8,128)(2,1)S(1)}, u32[]{:S(2)}, u32[]{:S(2)}) collective-permute-start(bf16[2,32,1024]{2,1,0:T(8,128)(2,1)S(1)} %get-tuple-element.15), channel_id=1, source_target_pairs={{0,8},{4,12},{8,0},{12,4},{16,24},{20,28},{24,16},{28,20},{1,9},{5... | collective-permute-start | bytes 393224 | tf_op jit(solution)/shard_map/ppermute | solution.py:169
  7.6 15.6 %collective-permute-start.9 = (bf16[2,32,1024]{2,1,0:T(8,128)(2,1)S(1)}, bf16[2,32,1024]{2,1,0:T(8,128)(2,1)S(1)}, u32[]{:S(2)}, u32[]{:S(2)}) collective-permute-start(bf16[2,32,1024]{2,1,0:T(8,128)(2,1)S(1)} %get-tuple-element.16), channel_id=1, source_target_pairs={{0,12},{4,8},{8,4},{12,0},{16,28},{20,24},{24,20},{28,16},{1,13},{... | collective-permute-start | bytes 393224 | tf_op jit(solution)/shard_map/ppermute | solution.py:169
  7.7 19.1 %collective-permute-start.10 = (bf16[2,32,1024]{2,1,0:T(8,128)(2,1)S(1)}, bf16[2,32,1024]{2,1,0:T(8,128)(2,1)S(1)}, u32[]{:S(2)}, u32[]{:S(2)}) collective-permute-start(bf16[2,32,1024]{2,1,0:T(8,128)(2,1)S(1)} %get-tuple-element.17), channel_id=1, source_target_pairs={{0,16},{4,20},{8,24},{12,28},{16,0},{20,4},{24,8},{28,12},{1,17},{... | collective-permute-start | bytes 393224 | tf_op jit(solution)/shard_map/ppermute | solution.py:169
  9.5 18.6 %collective-permute-start.11 = (bf16[2,32,1024]{2,1,0:T(8,128)(2,1)S(1)}, bf16[2,32,1024]{2,1,0:T(8,128)(2,1)S(1)}, u32[]{:S(2)}, u32[]{:S(2)}) collective-permute-start(bf16[2,32,1024]{2,1,0:T(8,128)(2,1)S(1)} %get-tuple-element.18), channel_id=1, source_target_pairs={{0,20},{4,16},{8,28},{12,24},{16,4},{20,0},{24,12},{28,8},{1,21},{... | collective-permute-start | bytes 393224 | tf_op jit(solution)/shard_map/ppermute | solution.py:169
  9.5 19.9 %collective-permute-start.12 = (bf16[2,32,1024]{2,1,0:T(8,128)(2,1)S(1)}, bf16[2,32,1024]{2,1,0:T(8,128)(2,1)S(1)}, u32[]{:S(2)}, u32[]{:S(2)}) collective-permute-start(bf16[2,32,1024]{2,1,0:T(8,128)(2,1)S(1)} %get-tuple-element.19), channel_id=1, source_target_pairs={{0,24},{4,28},{8,16},{12,20},{16,8},{20,12},{24,0},{28,4},{1,25},{... | collective-permute-start | bytes 393224 | tf_op jit(solution)/shard_map/ppermute | solution.py:169
  12.1 17.3 %collective-permute-start.13 = (bf16[2,32,1024]{2,1,0:T(8,128)(2,1)S(1)}, bf16[2,32,1024]{2,1,0:T(8,128)(2,1)S(1)}, u32[]{:S(2)}, u32[]{:S(2)}) collective-permute-start(bf16[2,32,1024]{2,1,0:T(8,128)(2,1)S(1)} %get-tuple-element.20), channel_id=1, source_target_pairs={{0,28},{4,24},{8,20},{12,16},{16,12},{20,8},{24,4},{28,0},{1,29},{... | collective-permute-start | bytes 393224 | tf_op jit(solution)/shard_map/ppermute | solution.py:169
  23.3 40.2 %collective-permute-start.6 = (bf16[64,1024]{1,0:T(8,128)(2,1)S(1)}, bf16[64,1024]{1,0:T(8,128)(2,1)S(1)}, u32[]{:S(2)}, u32[]{:S(2)}) collective-permute-start(bf16[64,1024]{1,0:T(8,128)(2,1)S(1)} %product.8), channel_id=1, source_target_pairs={{0,1},{3,2},{4,5},{7,6},{8,9},{11,10},{12,13},{15,14},{16,17},{19,... | collective-permute-start | bytes 393224 | tf_op jit(solution)/shard_map/ppermute | solution.py:119
  26.8 22.2 %collective-permute-start.1 = (bf16[64,1024]{1,0:T(8,128)(2,1)S(1)}, bf16[64,1024]{1,0:T(8,128)(2,1)S(1)}, u32[]{:S(2)}, u32[]{:S(2)}) collective-permute-start(bf16[64,1024]{1,0:T(8,128)(2,1)S(1)} %product.10), channel_id=1, source_target_pairs={{0,1},{3,2},{4,5},{7,6},{8,9},{11,10},{12,13},{15,14},{16,17},{19,... | collective-permute-start | bytes 393224 | tf_op jit(solution)/shard_map/ppermute | solution.py:119
  28.1 22.3 %collective-permute-start.4 = (bf16[64,1024]{1,0:T(8,128)(2,1)S(1)}, bf16[64,1024]{1,0:T(8,128)(2,1)S(1)}, u32[]{:S(2)}, u32[]{:S(2)}) collective-permute-start(bf16[64,1024]{1,0:T(8,128)(2,1)S(1)} %product.11), channel_id=1, source_target_pairs={{0,1},{3,2},{4,5},{7,6},{8,9},{11,10},{12,13},{15,14},{16,17},{19,... | collective-permute-start | bytes 393224 | tf_op jit(solution)/shard_map/ppermute | solution.py:119
  32.9 36.3 %collective-permute-start.19 = (bf16[192,1024]{1,0:T(8,128)(2,1)S(1)}, bf16[192,1024]{1,0:T(8,128)(2,1)S(1)}, u32[]{:S(2)}, u32[]{:S(2)}) collective-permute-start(bf16[192,1024]{1,0:T(8,128)(2,1)S(1)} %product.12), channel_id=1, source_target_pairs={{0,1},{3,2},{4,5},{7,6},{8,9},{11,10},{12,13},{15,14},{16,17},{19,... | collective-permute-start | bytes 1179656 | tf_op jit(solution)/shard_map/ppermute | solution.py:119
  37.6 15.2 %collective-permute-start.14 = (bf16[192,1024]{1,0:T(8,128)(2,1)S(1)}, bf16[192,1024]{1,0:T(8,128)(2,1)S(1)}, u32[]{:S(2)}, u32[]{:S(2)}) collective-permute-start(bf16[192,1024]{1,0:T(8,128)(2,1)S(1)} %product.14), channel_id=1, source_target_pairs={{0,1},{3,2},{4,5},{7,6},{8,9},{11,10},{12,13},{15,14},{16,17},{19,... | collective-permute-start | bytes 1179656 | tf_op jit(solution)/shard_map/ppermute | solution.py:119
  45.6 49.9 %copy-start.2 = (s32[8]{0:T(128)S(1)}, s32[8]{0:T(128)}, u32[]{:S(2)}) copy-start(s32[8]{0:T(128)} %q_owner.3) | copy-start | bytes 100
  49.0 12.2 %collective-permute-start.17 = (bf16[192,1024]{1,0:T(8,128)(2,1)S(1)}, bf16[192,1024]{1,0:T(8,128)(2,1)S(1)}, u32[]{:S(2)}, u32[]{:S(2)}) collective-permute-start(bf16[192,1024]{1,0:T(8,128)(2,1)S(1)} %product.15), channel_id=1, source_target_pairs={{0,1},{3,2},{4,5},{7,6},{8,9},{11,10},{12,13},{15,14},{16,17},{19,... | collective-permute-start | bytes 1179656 | tf_op jit(solution)/shard_map/ppermute | solution.py:119
  50.4 3.2 %collective-permute-start.2 = (bf16[64,1024]{1,0:T(8,128)(2,1)S(1)}, bf16[64,1024]{1,0:T(8,128)(2,1)S(1)}, u32[]{:S(2)}, u32[]{:S(2)}) collective-permute-start(bf16[64,1024]{1,0:T(8,128)(2,1)S(1)} %add_convert_fusion.7), channel_id=1, source_target_pairs={{1,2},{2,1},{5,6},{6,5},{9,10},{10,9},{13,14},{14,13},{17,18},{18,... | collective-permute-start | bytes 393224 | tf_op jit(solution)/shard_map/ppermute | solution.py:119
  52.8 12.0 %collective-permute-start.5 = (bf16[64,1024]{1,0:T(8,128)(2,1)S(1)}, bf16[64,1024]{1,0:T(8,128)(2,1)S(1)}, u32[]{:S(2)}, u32[]{:S(2)}) collective-permute-start(bf16[64,1024]{1,0:T(8,128)(2,1)S(1)} %add_convert_fusion.5), channel_id=1, source_target_pairs={{1,2},{2,1},{5,6},{6,5},{9,10},{10,9},{13,14},{14,13},{17,18},{18,... | collective-permute-start | bytes 393224 | tf_op jit(solution)/shard_map/ppermute | solution.py:119
  53.6 9.0 %collective-permute-start.15 = (bf16[192,1024]{1,0:T(8,128)(2,1)S(1)}, bf16[192,1024]{1,0:T(8,128)(2,1)S(1)}, u32[]{:S(2)}, u32[]{:S(2)}) collective-permute-start(bf16[192,1024]{1,0:T(8,128)(2,1)S(1)} %add_convert_fusion.3), channel_id=1, source_target_pairs={{1,2},{2,1},{5,6},{6,5},{9,10},{10,9},{13,14},{14,13},{17,18},{18,... | collective-permute-start | bytes 1179656 | tf_op jit(solution)/shard_map/ppermute | solution.py:119
  61.2 7.7 %collective-permute-start.3 = (bf16[64,1024]{1,0:T(8,128)(2,1)S(1)}, bf16[64,1024]{1,0:T(8,128)(2,1)S(1)}, u32[]{:S(2)}, u32[]{:S(2)}) collective-permute-start(bf16[64,1024]{1,0:T(8,128)(2,1)S(1)} %add_convert_fusion.6), channel_id=1, source_target_pairs={{2,3},{1,0},{6,7},{5,4},{10,11},{9,8},{14,15},{13,12},{18,19},{17,... | collective-permute-start | bytes 393224 | tf_op jit(solution)/shard_map/ppermute | solution.py:119
  62.6 6.5 %collective-permute-start.18 = (bf16[192,1024]{1,0:T(8,128)(2,1)S(1)}, bf16[192,1024]{1,0:T(8,128)(2,1)S(1)}, u32[]{:S(2)}, u32[]{:S(2)}) collective-permute-start(bf16[192,1024]{1,0:T(8,128)(2,1)S(1)} %add_convert_fusion.1), channel_id=1, source_target_pairs={{1,2},{2,1},{5,6},{6,5},{9,10},{10,9},{13,14},{14,13},{17,18},{18,... | collective-permute-start | bytes 1179656 | tf_op jit(solution)/shard_map/ppermute | solution.py:119
  63.5 22.1 %collective-permute-start.16 = (bf16[192,1024]{1,0:T(8,128)(2,1)S(1)}, bf16[192,1024]{1,0:T(8,128)(2,1)S(1)}, u32[]{:S(2)}, u32[]{:S(2)}) collective-permute-start(bf16[192,1024]{1,0:T(8,128)(2,1)S(1)} %add_convert_fusion.2), channel_id=1, source_target_pairs={{2,3},{1,0},{6,7},{5,4},{10,11},{9,8},{14,15},{13,12},{18,19},{17,... | collective-permute-start | bytes 1179656 | tf_op jit(solution)/shard_map/ppermute | solution.py:119
  69.0 21.4 %collective-permute-start.7 = (bf16[32,1024]{1,0:T(8,128)(2,1)S(1)}, bf16[32,1024]{1,0:T(8,128)(2,1)S(1)}, u32[]{:S(2)}, u32[]{:S(2)}) collective-permute-start(bf16[32,1024]{1,0:T(8,128)(2,1)S(1)} %get-tuple-element.27), channel_id=1, source_target_pairs={{0,4},{4,0},{8,12},{12,8},{16,20},{20,16},{24,28},{28,24},{1,5},{5... | collective-permute-start | bytes 196616 | tf_op jit(solution)/shard_map/ppermute | solution.py:169
  85.9 4.8 %collective-permute-start.25 = (bf16[32,1024]{1,0:T(8,128)(2,1)S(1)}, bf16[32,1024]{1,0:T(8,128)(2,1)S(1)}, u32[]{:S(2)}, u32[]{:S(2)}) collective-permute-start(bf16[32,1024]{1,0:T(8,128)(2,1)S(1)} %get-tuple-element.21), channel_id=1, source_target_pairs={{0,28},{4,24},{8,20},{12,16},{16,12},{20,8},{24,4},{28,0},{1,29},{... | collective-permute-start | bytes 196616 | tf_op jit(solution)/shard_map/ppermute | solution.py:169
  86.0 6.0 %collective-permute-start.24 = (bf16[32,1024]{1,0:T(8,128)(2,1)S(1)}, bf16[32,1024]{1,0:T(8,128)(2,1)S(1)}, u32[]{:S(2)}, u32[]{:S(2)}) collective-permute-start(bf16[32,1024]{1,0:T(8,128)(2,1)S(1)} %get-tuple-element.22), channel_id=1, source_target_pairs={{0,24},{4,28},{8,16},{12,20},{16,8},{20,12},{24,0},{28,4},{1,25},{... | collective-permute-start | bytes 196616 | tf_op jit(solution)/shard_map/ppermute | solution.py:169
  87.6 5.7 %collective-permute-start.23 = (bf16[32,1024]{1,0:T(8,128)(2,1)S(1)}, bf16[32,1024]{1,0:T(8,128)(2,1)S(1)}, u32[]{:S(2)}, u32[]{:S(2)}) collective-permute-start(bf16[32,1024]{1,0:T(8,128)(2,1)S(1)} %get-tuple-element.23), channel_id=1, source_target_pairs={{0,20},{4,16},{8,28},{12,24},{16,4},{20,0},{24,12},{28,8},{1,21},{... | collective-permute-start | bytes 196616 | tf_op jit(solution)/shard_map/ppermute | solution.py:169
  88.9 5.9 %collective-permute-start.22 = (bf16[32,1024]{1,0:T(8,128)(2,1)S(1)}, bf16[32,1024]{1,0:T(8,128)(2,1)S(1)}, u32[]{:S(2)}, u32[]{:S(2)}) collective-permute-start(bf16[32,1024]{1,0:T(8,128)(2,1)S(1)} %get-tuple-element.24), channel_id=1, source_target_pairs={{0,16},{4,20},{8,24},{12,28},{16,0},{20,4},{24,8},{28,12},{1,17},{... | collective-permute-start | bytes 196616 | tf_op jit(solution)/shard_map/ppermute | solution.py:169
  90.4 4.4 %collective-permute-start.21 = (bf16[32,1024]{1,0:T(8,128)(2,1)S(1)}, bf16[32,1024]{1,0:T(8,128)(2,1)S(1)}, u32[]{:S(2)}, u32[]{:S(2)}) collective-permute-start(bf16[32,1024]{1,0:T(8,128)(2,1)S(1)} %get-tuple-element.25), channel_id=1, source_target_pairs={{0,12},{4,8},{8,4},{12,0},{16,28},{20,24},{24,20},{28,16},{1,13},{... | collective-permute-start | bytes 196616 | tf_op jit(solution)/shard_map/ppermute | solution.py:169
  90.7 4.8 %collective-permute-start.20 = (bf16[32,1024]{1,0:T(8,128)(2,1)S(1)}, bf16[32,1024]{1,0:T(8,128)(2,1)S(1)}, u32[]{:S(2)}, u32[]{:S(2)}) collective-permute-start(bf16[32,1024]{1,0:T(8,128)(2,1)S(1)} %get-tuple-element.26), channel_id=1, source_target_pairs={{0,8},{4,12},{8,0},{12,4},{16,24},{20,28},{24,16},{28,20},{1,9},{5... | collective-permute-start | bytes 196616 | tf_op jit(solution)/shard_map/ppermute | solution.py:169
